TPU v7x, 32 devices: a whole 2x2x4 slice. The times are simulated.
32 devices in a mesh: blk: 8 (over z, x), freq: 4 (over y, core).
Axes of the slice: x: 2, y: 2, z: 4, core: 2. Of those that a mesh axis runs over, the one named last changes fastest.
Arguments:
- spectra: bfloat16 [2, 128, 1024, 512], P(None, 'freq', 'blk'), may hold values from -6 to 6
- halfwidth: int32 [1024], P('blk'), may hold values from 1 to 3
Outputs:
- cross: bfloat16 [2, 2, 128, 1024, 128], P(None, None, 'freq', 'blk')
All inputs are finite; a program needn't handle non-finite values.
Results may differ from a plain program's by a relative error of at most 0.0064.
Values may be sent and summed in bfloat16 or wider, within the bound.
A program may use at most 128 MiB of HBM per device.

v0:
```python
import jax
import jax.numpy as jnp
from jax import lax
from jax.sharding import PartitionSpec as P

W = 512
F = 128
HMAX = 3
ROUNDS = 2


def with_halo(block, sides, width):
    for axis, dim in sides:
        count = lax.axis_size(axis)
        forward = [(i, i + 1) for i in range(count - 1)]
        backward = [(target, source) for source, target in forward]
        low = lax.ppermute(
            lax.slice_in_dim(block, block.shape[dim] - width, None, axis=dim), axis, forward
        )
        high = lax.ppermute(lax.slice_in_dim(block, 0, width, axis=dim), axis, backward)
        block = jnp.concatenate([low, block, high], axis=dim)
    return block


def partner_2(value, axis, apart):
    return lax.ppermute(value, axis, [(i, i ^ 1 << apart) for i in range(lax.axis_size(axis))])


def whiten_block(spectra, halfwidth):
    real_part = spectra[0].astype(jnp.float32)
    imag_part = spectra[1].astype(jnp.float32)
    energy = real_part * real_part + imag_part * imag_part
    bin_count = energy.shape[0]
    padded = with_halo(energy, (("freq", 0),), HMAX)
    global_bin = lax.axis_index("freq") * bin_count + jnp.arange(bin_count, dtype=jnp.int32)
    smooth = jnp.zeros_like(energy)
    counts = jnp.zeros(energy.shape[:2], jnp.float32)
    for offset in range(-HMAX, HMAX + 1):
        inside = abs(offset) <= halfwidth
        in_grid = (global_bin + offset >= 0) & (global_bin + offset < F)
        weight = (inside[None, :] & in_grid[:, None]).astype(jnp.float32)
        smooth = smooth + weight[:, :, None] * padded[offset + HMAX : offset + HMAX + bin_count]
        counts = counts + weight
    root_mean = jnp.sqrt(smooth / counts[:, :, None])
    factor = 1.0 / jnp.maximum(root_mean, 0.5)
    return jnp.stack((real_part * factor, imag_part * factor)).astype(jnp.bfloat16)


def cross_sums(own_block, partner):
    real_sum = jnp.einsum(
        "fcw,fdw->fcd", own_block[0], partner[0], preferred_element_type=jnp.float32
    )
    real_sum = real_sum + jnp.einsum(
        "fcw,fdw->fcd", own_block[1], partner[1], preferred_element_type=jnp.float32
    )
    imag_sum = jnp.einsum(
        "fcw,fdw->fcd", own_block[1], partner[0], preferred_element_type=jnp.float32
    )
    imag_sum = imag_sum - jnp.einsum(
        "fcw,fdw->fcd", own_block[0], partner[1], preferred_element_type=jnp.float32
    )
    return jnp.stack((real_sum, imag_sum)).astype(jnp.bfloat16)


def per_device(spectra, halfwidth):
    whitened = whiten_block(spectra, halfwidth)
    block_count = lax.axis_size("blk")
    position = lax.axis_index("blk")
    top_bit = block_count.bit_length() - 1
    half_len = W // 2
    tile_list = []
    for round_index in range(ROUNDS):
        mask_bit = top_bit - 1 - round_index
        side_bit = position >> mask_bit & 1
        own_start = side_bit * half_len
        give_start = (1 - side_bit) * half_len
        own_half = lax.dynamic_slice_in_dim(whitened, own_start, half_len, 3)
        sent_half = lax.dynamic_slice_in_dim(whitened, give_start, half_len, 3)
        taken = partner_2(sent_half, "blk", mask_bit)
        partial_value = cross_sums(own_half, taken)
        returned = partner_2(partial_value, "blk", mask_bit)
        mirrored = jnp.stack(
            (
                jnp.transpose(returned[0], (0, 2, 1)).astype(jnp.float32),
                -jnp.transpose(returned[1], (0, 2, 1)).astype(jnp.float32),
            )
        )
        summed = partial_value.astype(jnp.float32) + mirrored
        tile_list.append((summed * W ** (-0.5)).astype(jnp.bfloat16))
    return jnp.stack(tile_list)


def solution(mesh):
    return jax.shard_map(
        per_device,
        mesh=mesh,
        in_specs=(P(None, "freq", "blk", None), P("blk")),
        out_specs=P(None, None, "freq", "blk", None),
        check_vma=False,
    )
```

profile of v0, /device:TPU:0, one launch (start us, length us, event | category | flops | bytes accessed | tf_op | source)
XLA Modules:
  0.0 355.6 jit_solution(4371389985174693837)
XLA Ops:
  0.0 4.3 %fusion.16 = f32[32,128,512]{2,1,0:T(8,128)S(1)} fusion(bf16[2,32,128,512]{3,2,1,0:T(8,128)(2,1)} %param.2), kind=kLoop, calls=%fused_computation.36 | loop fusion | flops 10485760 | bytes 16777216 | tf_op jit(solution)/shard_map/add | solution.py:32
  4.3 3.3 copy-done
  7.8 2.4 collective-permute-start
  12.0 4.4 %collective-permute-done.1 = f32[3,128,512]{2,1,0:T(8,128)S(1)} collective-permute-done((f32[3,128,512]{2,1,0:T(8,128)S(1)}, f32[3,128,512]{2,1,0:T(8,128)S(1)}, u32[]{:S(2)}, u32[]{:S(2)}) %collective-permute-start.1) | collective-permute-done | bytes 786464 | tf_op jit(solution)/shard_map/ppermute | solution.py:20
  16.4 24.4 %fusion.21 = (bf16[1,32,128,512]{3,2,1,0:T(8,128)(2,1)}, f32[32,128,512]{2,1,0:T(8,128)}) fusion(bf16[2,32,128,512]{3,2,1,0:T(8,128)(2,1)} %param.2, f32[32,128]{1,0:T(8,128)S(1)} %add_add_fusion, f32[3,128,512]{2,1,0:T(8,128)S(1)} %collective-permute-done.1, f32[32,128,512]{2,1,0:T(8,128)} %copy-done, f32[32,128]{1,0:T(8,128)S(1)} %get-tuple-element.14, ...), kind=kLoop, calls=%fused_computation.44 | loop fusion | flops 52428800 | bytes 26869760 | tf_op jit(solution)/shard_map/stack | solution.py:46
  40.9 6.4 %fusion.22 = bf16[1,32,128,512]{3,2,1,0:T(8,128)(2,1)S(1)} fusion(f32[32,128,512]{2,1,0:T(8,128)} %get-tuple-element.6, bf16[2,32,128,512]{3,2,1,0:T(8,128)(2,1)} %param.2), kind=kLoop, calls=%fused_computation.45 | loop fusion | flops 6291456 | bytes 16777216 | tf_op jit(solution)/shard_map/stack | solution.py:46
  47.3 4.4 %fusion.25 = (bf16[2,32,128,256]{3,2,1,0:T(8,128)(2,1)}, bf16[2,32,128,256]{3,2,1,0:T(8,128)(2,1)S(1)}, bf16[2,32,128,256]{3,2,1,0:T(8,128)(2,1)S(1)}, bf16[2,32,128,256]{3,2,1,0:T(8,128)(2,1)}) fusion(s32[]{:T(128)S(6)} %select_n.13, bf16[1,32,128,512]{3,2,1,0:T(8,128)(2,1)S(1)} %fusion.22, bf16[1,32,128,512]{3,2,1,0:T(8,128)(2,1)S(1)} %copy-done.4, ...), kind=kLoop, calls=%fused_computation.48 | loop fusion | flops 33554432 | bytes 25165840 | tf_op jit(solution)/shard_map/stack | solution.py:46
  51.6 1.6 collective-permute-start.4
  53.2 2.6 collective-permute-start.2
  55.8 176.3 %collective-permute-done.4 = bf16[2,32,128,256]{3,2,1,0:T(8,128)(2,1)S(1)} collective-permute-done((bf16[2,32,128,256]{3,2,1,0:T(8,128)(2,1)}, bf16[2,32,128,256]{3,2,1,0:T(8,128)(2,1)S(1)}, u32[]{:S(2)}, u32[]{:S(2)}) %collective-permute-start.4) | collective-permute-done | bytes 4194336 | tf_op jit(solution)/shard_map/ppermute | solution.py:26
  235.0 1.5 pad_maximum_fusion.4
  240.0 3.1 fusion.34
  243.4 2.4 add_convert_fusion.1
  245.8 1.6 pad_maximum_fusion.3
  247.4 4.2 %collective-permute-start.3 = (bf16[2,32,128,128]{3,2,1,0:T(8,128)(2,1)}, bf16[2,32,128,128]{3,2,1,0:T(8,128)(2,1)}, u32[]{:S(2)}, u32[]{:S(2)}) collective-permute-start(bf16[2,32,128,128]{3,2,1,0:T(8,128)(2,1)} %pad_maximum_fusion.3), channel_id=1, source_target_pairs={{0,16},{4,20},{8,24},{12,28},{16,0},{20,4},{24,8},{28,12},{1,17},{... | collective-permute-start | bytes 6291464 | tf_op jit(solution)/shard_map/ppermute | solution.py:26
  252.9 2.3 maximum_convert_fusion
  255.2 5.6 %copy.12 = f32[1,2,32,128,128]{3,4,2,1,0:T(8,128)} copy(f32[1,2,32,128,128]{4,3,2,1,0:T(8,128)} %maximum_convert_fusion) | data formatting | bytes 8388608 | tf_op jit(solution)/shard_map/convert_element_type | solution.py:88
  260.8 56.6 %collective-permute-done.5 = bf16[2,32,128,128]{3,2,1,0:T(8,128)(2,1)} collective-permute-done((bf16[2,32,128,128]{3,2,1,0:T(8,128)(2,1)}, bf16[2,32,128,128]{3,2,1,0:T(8,128)(2,1)}, u32[]{:S(2)}, u32[]{:S(2)}) %collective-permute-start.5) | collective-permute-done | bytes 2097184 | tf_op jit(solution)/shard_map/ppermute | solution.py:26
  318.8 1.5 convert_bitcast_fusion
  321.3 21.8 %collective-permute-done.3 = bf16[2,32,128,128]{3,2,1,0:T(8,128)(2,1)} collective-permute-done((bf16[2,32,128,128]{3,2,1,0:T(8,128)(2,1)}, bf16[2,32,128,128]{3,2,1,0:T(8,128)(2,1)}, u32[]{:S(2)}, u32[]{:S(2)}) %collective-permute-start.3) | collective-permute-done | bytes 2097184 | tf_op jit(solution)/shard_map/ppermute | solution.py:26
  343.1 1.5 negate_bitcast_fusion.1
  344.6 1.5 convert_bitcast_fusion.1
  347.0 2.3 pad_maximum_fusion.2
  349.3 6.3 %copy.13 = bf16[2,2,32,128,128]{4,3,2,1,0:T(8,128)(2,1)} copy(bf16[2,2,32,128,128]{3,4,2,1,0:T(8,128)(2,1)} %pad_maximum_fusion.2) | data formatting | bytes 8388608 | tf_op jit(solution)/shard_map/stack | solution.py:90
  (47 shorter events, 13.3 us)
Async XLA Ops:
  0.0 11.5 %copy-start.10 = (s32[128]{0:T(128)S(1)}, s32[128]{0:T(128)}, u32[]{:S(2)}) copy-start(s32[128]{0:T(128)} %param.3) | copy-start | bytes 1540
  4.3 3.3 copy-start
  7.8 4.3 %collective-permute-start = (f32[3,128,512]{2,1,0:T(8,128)S(1)}, f32[3,128,512]{2,1,0:T(8,128)S(1)}, u32[]{:S(2)}, u32[]{:S(2)}) collective-permute-start(f32[3,128,512]{2,1,0:T(8,128)S(1)} %get-tuple-element.11), channel_id=1, source_target_pairs={{0,1},{1,2},{2,3},{4,5},{5,6},{6,7},{8,9},{9,10},{10,11},{12,13},{... | collective-permute-start | bytes 2359304 | tf_op jit(solution)/shard_map/ppermute | solution.py:17
  10.2 6.3 %collective-permute-start.1 = (f32[3,128,512]{2,1,0:T(8,128)S(1)}, f32[3,128,512]{2,1,0:T(8,128)S(1)}, u32[]{:S(2)}, u32[]{:S(2)}) collective-permute-start(f32[3,128,512]{2,1,0:T(8,128)S(1)} %get-tuple-element.12), channel_id=1, source_target_pairs={{1,0},{2,1},{3,2},{5,4},{6,5},{7,6},{9,8},{10,9},{11,10},{13,12},{... | collective-permute-start | bytes 2359304 | tf_op jit(solution)/shard_map/ppermute | solution.py:20
  40.9 6.4 %copy-start.4 = (bf16[1,32,128,512]{3,2,1,0:T(8,128)(2,1)S(1)}, bf16[1,32,128,512]{3,2,1,0:T(8,128)(2,1)}, u32[]{:S(2)}) copy-start(bf16[1,32,128,512]{3,2,1,0:T(8,128)(2,1)} %get-tuple-element.5) | copy-start | bytes 12582916
  51.6 185.7 %copy-start.1 = (bf16[2,32,128,256]{3,2,1,0:T(8,128)(2,1)}, bf16[2,32,128,256]{3,2,1,0:T(8,128)(2,1)S(1)}, u32[]{:S(2)}) copy-start(bf16[2,32,128,256]{3,2,1,0:T(8,128)(2,1)S(1)} %get-tuple-element.8) | copy-start | bytes 12582916
  51.6 180.5 %collective-permute-start.4 = (bf16[2,32,128,256]{3,2,1,0:T(8,128)(2,1)}, bf16[2,32,128,256]{3,2,1,0:T(8,128)(2,1)S(1)}, u32[]{:S(2)}, u32[]{:S(2)}) collective-permute-start(bf16[2,32,128,256]{3,2,1,0:T(8,128)(2,1)} %get-tuple-element.10), channel_id=1, source_target_pairs={{0,8},{4,12},{8,0},{12,4},{16,24},{20,28},{24,16},{28,20},{1,9},{5... | collective-permute-start | bytes 12582920 | tf_op jit(solution)/shard_map/ppermute | solution.py:26
  53.2 183.4 %collective-permute-start.2 = (bf16[2,32,128,256]{3,2,1,0:T(8,128)(2,1)}, bf16[2,32,128,256]{3,2,1,0:T(8,128)(2,1)S(1)}, u32[]{:S(2)}, u32[]{:S(2)}) collective-permute-start(bf16[2,32,128,256]{3,2,1,0:T(8,128)(2,1)} %get-tuple-element.7), channel_id=1, source_target_pairs={{0,16},{4,20},{8,24},{12,28},{16,0},{20,4},{24,8},{28,12},{1,17},{... | collective-permute-start | bytes 12582920 | tf_op jit(solution)/shard_map/ppermute | solution.py:26
  236.6 80.8 %collective-permute-start.5 = (bf16[2,32,128,128]{3,2,1,0:T(8,128)(2,1)}, bf16[2,32,128,128]{3,2,1,0:T(8,128)(2,1)}, u32[]{:S(2)}, u32[]{:S(2)}) collective-permute-start(bf16[2,32,128,128]{3,2,1,0:T(8,128)(2,1)} %pad_maximum_fusion.4), channel_id=1, source_target_pairs={{0,8},{4,12},{8,0},{12,4},{16,24},{20,28},{24,16},{28,20},{1,9},{5... | collective-permute-start | bytes 6291464 | tf_op jit(solution)/shard_map/ppermute | solution.py:26
  236.6 2.0 copy-start.3
  238.6 1.4 copy-start.6
  240.0 3.4 copy-start.2
  243.4 2.4 copy-start.8
  247.4 95.7 %collective-permute-start.3 = (bf16[2,32,128,128]{3,2,1,0:T(8,128)(2,1)}, bf16[2,32,128,128]{3,2,1,0:T(8,128)(2,1)}, u32[]{:S(2)}, u32[]{:S(2)}) collective-permute-start(bf16[2,32,128,128]{3,2,1,0:T(8,128)(2,1)} %pad_maximum_fusion.3), channel_id=1, source_target_pairs={{0,16},{4,20},{8,24},{12,28},{16,0},{20,4},{24,8},{28,12},{1,17},{... | collective-permute-start | bytes 6291464 | tf_op jit(solution)/shard_map/ppermute | solution.py:26
  260.8 59.5 %copy-start.5 = (f32[1,2,32,128,128]{3,4,2,1,0:T(8,128)S(1)}, f32[1,2,32,128,128]{3,4,2,1,0:T(8,128)}, u32[]{:S(2)}) copy-start(f32[1,2,32,128,128]{3,4,2,1,0:T(8,128)} %copy.12) | copy-start | bytes 12582916
  321.3 24.8 %copy-start.7 = (bf16[32,128,128]{1,2,0:T(8,128)(2,1)S(1)}, bf16[32,128,128]{1,2,0:T(8,128)(2,1)}, u32[]{:S(2)}) copy-start(bf16[32,128,128]{1,2,0:T(8,128)(2,1)} %copy-done.6) | copy-start | bytes 3145732
  321.3 24.8 %copy-start.9 = (bf16[1,1,32,128,128]{3,4,2,1,0:T(8,128)(2,1)S(1)}, bf16[1,1,32,128,128]{3,4,2,1,0:T(8,128)(2,1)}, u32[]{:S(2)}) copy-start(bf16[1,1,32,128,128]{3,4,2,1,0:T(8,128)(2,1)} %copy.10) | copy-start | bytes 3145732
where the time goes:
time: 356 us
  waiting for transfers between devices  259 us (73%)
  other arithmetic  55.2 us (16%)
  local copies, waits for them, and re-layouts  19.1 us (5%)
  starting transfers between devices  12 us (3%)
  matrix products  9.78 us (3%)
    ppermute x4, waiting for transfers between devices, partner_2(): lax.ppermute(value, axis, [(i, i ^ 1 << apart) for i in range(lax.axis_si...  255 us
    another operation x3, other arithmetic, whiten_block(): jnp.stack((real_part * factor, imag_part * factor)).astype(jnp.bfloat16)  35.2 us
    ppermute x4, starting transfers between devices, partner_2(): lax.ppermute(value, axis, [(i, i ^ 1 << apart) for i in range(lax.axis_si...  8.34 us
  transfers between devices with their start and end apart: 6, of which 4 were waited for; matrix products, arithmetic and copies ran while one was open for 8% of the time, Pallas kernels for 0%

commit v1 on v0

v1 whole, which is shorter than its diff:
```python
import jax
import jax.numpy as jnp
from jax import lax
from jax.experimental import pallas as pl
from jax.experimental.pallas import tpu as pltpu
from jax.sharding import PartitionSpec as P

HMAX = 3
ROUNDS = 2
STEP = 2
ROWS = 16
LANES = 128


def cross_kernel(
    spectra, widths, out, energy, whitened, taken, own_tiles, sent_tiles,
    halo_send, halo_recv, x_send, x_recv, t_send, t_recv, o_sem,
):
    _, bins, channels, windows = spectra.shape
    half = bins // 2
    chunks = half // STEP
    fresh_chunks = (half - 2 * HMAX) // STEP
    first_edge_chunk = (half - HMAX) // STEP
    row_blocks = channels // ROWS
    scale = windows ** -0.5

    block = lax.axis_index("blk")
    block_count = lax.axis_size("blk")
    freq = lax.axis_index("freq")
    freq_count = lax.axis_size("freq")
    bin_total = bins * freq_count
    has_low = freq > 0
    has_high = freq < freq_count - 1

    partners = []
    mine = 0
    for round_index in range(ROUNDS):
        flip = block_count >> (round_index + 1)
        side = (block // flip) % 2
        partners.append(block + flip * (1 - 2 * side))
        mine = mine + side
    mine = mine % 2
    given = 1 - mine

    def chunk_start(which, chunk):
        return (half - STEP * (chunk + 1)) + which * (STEP * (2 * chunk + 1))

    def make_energy(k):
        @pl.loop(0, row_blocks)
        def _(block_index):
            rows = pl.ds(pl.multiple_of(block_index * ROWS, ROWS), ROWS)
            real_part = spectra[0, k, rows, :].astype(jnp.float32)
            imag_part = spectra[1, k, rows, :].astype(jnp.float32)
            energy[k + HMAX, rows, :] = real_part * real_part + imag_part * imag_part

    def whiten(k):
        position = freq * bins + k
        inside = []
        for offset in range(1, HMAX + 1):
            low = (position - offset >= 0).astype(jnp.int32)
            high = (position + offset < bin_total).astype(jnp.int32)
            inside.append((low + high).astype(jnp.float32))

        @pl.loop(0, row_blocks)
        def _(block_index):
            rows = pl.ds(pl.multiple_of(block_index * ROWS, ROWS), ROWS)
            width = widths[rows, :]
            counts = jnp.ones((ROWS, LANES), jnp.float32)
            weights = []
            for offset in range(1, HMAX + 1):
                weight = (width >= offset).astype(jnp.float32)
                counts = counts + weight * inside[offset - 1]
                weights.append(weight)
            inverse = 1.0 / counts
            for lane in range(0, windows, LANES):
                lanes = pl.ds(lane, LANES)
                smooth = energy[k + HMAX, rows, lanes]
                for offset in range(1, HMAX + 1):
                    pair = (
                        energy[k + HMAX - offset, rows, lanes]
                        + energy[k + HMAX + offset, rows, lanes]
                    )
                    smooth = smooth + weights[offset - 1] * pair
                factor = lax.rsqrt(jnp.maximum(smooth * inverse, 0.25))
                for part in range(2):
                    value = spectra[part, k, rows, lanes].astype(jnp.float32)
                    whitened[part, k, rows, lanes] = (value * factor).astype(jnp.bfloat16)

    def halo_copy(side):
        source = (HMAX, bins)[side]
        target = (bins + HMAX, 0)[side]
        return pltpu.make_async_remote_copy(
            src_ref=energy.at[pl.ds(source, HMAX)],
            dst_ref=energy.at[pl.ds(target, HMAX)],
            send_sem=halo_send.at[side],
            recv_sem=halo_recv.at[1 - side],
            device_id={"freq": freq + (2 * side - 1)},
            device_id_type=pl.DeviceIdType.MESH,
        )

    def spectra_copy(r, chunk):
        return pltpu.make_async_remote_copy(
            src_ref=whitened.at[:, pl.ds(chunk_start(given, chunk), STEP)],
            dst_ref=taken.at[r, :, pl.ds(chunk * STEP, STEP)],
            send_sem=x_send.at[r, chunk],
            recv_sem=x_recv.at[r, chunk],
            device_id={"blk": partners[r]},
            device_id_type=pl.DeviceIdType.MESH,
        )

    def tile_copy(r, chunk, which):
        return pltpu.make_async_remote_copy(
            src_ref=sent_tiles.at[r, chunk],
            dst_ref=out.at[r, :, pl.ds(chunk_start(which, chunk), STEP)],
            send_sem=t_send.at[r, chunk],
            recv_sem=t_recv.at[r, chunk],
            device_id={"blk": partners[r]},
            device_id_type=pl.DeviceIdType.MESH,
        )

    def own_copy(r, chunk):
        return pltpu.make_async_copy(
            own_tiles.at[r, chunk],
            out.at[r, :, pl.ds(chunk_start(mine, chunk), STEP)],
            o_sem.at[r, chunk],
        )

    barrier = pltpu.get_barrier_semaphore()
    for partner in partners:
        pl.semaphore_signal(
            barrier, inc=1, device_id={"blk": partner}, device_id_type=pl.DeviceIdType.MESH
        )

    @pl.when(has_low)
    def _():
        pl.semaphore_signal(
            barrier, inc=1, device_id={"freq": freq - 1}, device_id_type=pl.DeviceIdType.MESH
        )

    @pl.when(has_high)
    def _():
        pl.semaphore_signal(
            barrier, inc=1, device_id={"freq": freq + 1}, device_id_type=pl.DeviceIdType.MESH
        )

    @pl.loop(0, HMAX)
    def _(index):
        make_energy(index)
        make_energy(bins - HMAX + index)

    pl.semaphore_wait(barrier, ROUNDS + has_low.astype(jnp.int32) + has_high.astype(jnp.int32))

    @pl.when(has_low)
    def _():
        halo_copy(0).start()

    @pl.when(jnp.logical_not(has_low))
    def _():
        energy[pl.ds(0, HMAX)] = jnp.zeros((HMAX, channels, windows), jnp.float32)

    @pl.when(has_high)
    def _():
        halo_copy(1).start()

    @pl.when(jnp.logical_not(has_high))
    def _():
        energy[pl.ds(bins + HMAX, HMAX)] = jnp.zeros((HMAX, channels, windows), jnp.float32)

    @pl.loop(half - HMAX, half + HMAX)
    def _(index):
        make_energy(index)

    def whiten_half(which, send):
        @pl.loop(0, chunks)
        def _(chunk):
            start = chunk_start(which, chunk)

            @pl.when(chunk < fresh_chunks)
            def _():
                for j in range(STEP):
                    make_energy(start + j + HMAX * (2 * which - 1))

            @pl.when((chunk == first_edge_chunk) & (which == 0) & has_low)
            def _():
                halo_copy(1).wait_recv()

            @pl.when((chunk == first_edge_chunk) & (which == 1) & has_high)
            def _():
                halo_copy(0).wait_recv()

            @pl.loop(0, STEP)
            def _(j):
                whiten(start + j)

            if send:
                for r in range(ROUNDS):
                    spectra_copy(r, chunk).start()

    whiten_half(given, True)
    whiten_half(mine, False)

    @pl.loop(0, chunks)
    def _(chunk):
        start = chunk_start(mine, chunk)
        for r in range(ROUNDS):
            spectra_copy(r, chunk).wait_recv()

            @pl.loop(0, STEP)
            def _(j):
                own = jnp.concatenate([whitened[0, start + j], whitened[1, start + j]], axis=0)
                other = jnp.concatenate(
                    [taken[r, 0, chunk * STEP + j], taken[r, 1, chunk * STEP + j]], axis=0
                )
                both = lax.dot_general(
                    own, other, (((1,), (1,)), ((), ())), preferred_element_type=jnp.float32
                )
                real_sum = both[:channels, :channels] + both[channels:, channels:]
                imag_sum = both[channels:, :channels] - both[:channels, channels:]
                real_sum = real_sum * scale
                imag_sum = imag_sum * scale
                own_tiles[r, chunk, 0, j] = real_sum.astype(jnp.bfloat16)
                own_tiles[r, chunk, 1, j] = imag_sum.astype(jnp.bfloat16)
                sent_tiles[r, chunk, 0, j] = real_sum.T.astype(jnp.bfloat16)
                sent_tiles[r, chunk, 1, j] = (-imag_sum.T).astype(jnp.bfloat16)

            tile_copy(r, chunk, mine).start()
            own_copy(r, chunk).start()

    @pl.when(has_low)
    def _():
        halo_copy(0).wait_send()

    @pl.when(has_high)
    def _():
        halo_copy(1).wait_send()

    @pl.loop(0, chunks)
    def _(chunk):
        for r in range(ROUNDS):
            spectra_copy(r, chunk).wait_send()
            own_copy(r, chunk).wait()
            tile_copy(r, chunk, mine).wait_send()
            tile_copy(r, chunk, given).wait_recv()


def per_device(spectra, halfwidth):
    _, bins, channels, windows = spectra.shape
    half = bins // 2
    chunks = half // STEP
    widths = jnp.broadcast_to(halfwidth[:, None], (channels, LANES))
    tiles = (ROUNDS, chunks, 2, STEP, channels, channels)
    dma = pltpu.SemaphoreType.DMA
    return pl.pallas_call(
        cross_kernel,
        out_shape=jax.ShapeDtypeStruct((ROUNDS, 2, bins, channels, channels), jnp.bfloat16),
        in_specs=[pl.BlockSpec(memory_space=pltpu.VMEM)] * 2,
        out_specs=pl.BlockSpec(memory_space=pl.ANY),
        scratch_shapes=[
            pltpu.VMEM((bins + 2 * HMAX, channels, windows), jnp.float32),
            pltpu.VMEM((2, bins, channels, windows), jnp.bfloat16),
            pltpu.VMEM((ROUNDS, 2, half, channels, windows), jnp.bfloat16),
            pltpu.VMEM(tiles, jnp.bfloat16),
            pltpu.VMEM(tiles, jnp.bfloat16),
            dma((2,)),
            dma((2,)),
            dma((ROUNDS, chunks)),
            dma((ROUNDS, chunks)),
            dma((ROUNDS, chunks)),
            dma((ROUNDS, chunks)),
            dma((ROUNDS, chunks)),
        ],
        compiler_params=pltpu.CompilerParams(
            collective_id=0, has_side_effects=True, vmem_limit_bytes=56 * 2**20
        ),
    )(spectra, widths)


def solution(mesh):
    return jax.shard_map(
        per_device,
        mesh=mesh,
        in_specs=(P(None, "freq", "blk", None), P("blk")),
        out_specs=P(None, None, "freq", "blk", None),
        check_vma=False,
    )
```

time: 356 us -> 244 us (0.69)
  waiting for transfers between devices: 259 us -> 0 us
  Pallas kernels: 0 us -> 237 us
  other arithmetic: 55.2 us -> 0 us
  local copies, waits for them, and re-layouts: 19.1 us -> 6.15 us
  starting transfers between devices: 12 us -> 0 us
  matrix products: 9.78 us -> 0 us
    ppermute x6 -> x0, waiting for transfers between devices: 259 us -> none  [the longest x4 255 us: partner_2(): lax.ppermute(value, axis, [(i, i ^ 1 << apart) for i in range(lax.axis_si...]
    pallas_call x0 -> x1, Pallas kernels: none -> 237 us  [per_device(): pl.pallas_call(cross_kernel, out_shape=jax.ShapeDtypeStruct((ROUNDS, 2, b...]
    another operation x10 -> x0, other arithmetic: 46.4 us -> none  [the longest x3 35.2 us: whiten_block(): jnp.stack((real_part * factor, imag_part * factor)).astype(jnp.bfloat16)]
    ppermute x6 -> x0, starting transfers between devices: 12 us -> none  [the longest x4 8.34 us: partner_2(): lax.ppermute(value, axis, [(i, i ^ 1 << apart) for i in range(lax.axis_si...]
    dot_general x8 -> x0, matrix products: 9.78 us -> none  [the longest x2 3.79 us: cross_sums(): jnp.einsum('fcw,fdw->fcd', own_block[1], partner[1], preferred_element_ty...]
    another operation x3 -> x0, local copies, waits for them, and re-layouts: 9.07 us -> none  [the longest x1 6.35 us: per_device(): return jnp.stack(tile_list)]
    convert_element_type x1 -> x0, local copies, waits for them, and re-layouts: 5.62 us -> none  [per_device(): summed = partial_value.astype(jnp.float32) + mirrored]
    convert_element_type x7 -> x0, other arithmetic: 4.43 us -> none  [the longest x1 2.28 us: per_device(): summed = partial_value.astype(jnp.float32) + mirrored]
  transfers between devices with their start and end apart: 6 -> 0, of which waited for: 4 -> 0; matrix products, arithmetic and copies ran while one was open for 8% -> 0% of each run, Pallas kernels for 0% -> 0%
where the time goes in v1:
time: 244 us
  Pallas kernels  237 us (97%)
  local copies, waits for them, and re-layouts  6.15 us (3%)
    pallas_call x1, Pallas kernels, per_device(): pl.pallas_call(cross_kernel, out_shape=jax.ShapeDtypeStruct((ROUNDS, 2, b...  237 us

profile of v1, /device:TPU:0, one launch (start us, length us, event | category | flops | bytes accessed | tf_op | source)
XLA Modules:
  0.0 243.6 jit_solution(1719984770258718384)
XLA Ops:
  0.0 1.4 broadcast_in_dim.2.widths
  1.4 237.4 %shard_map.28 = bf16[2,2,32,128,128]{4,3,2,1,0:T(8,128)(2,1)} custom-call(bf16[2,32,128,512]{3,2,1,0:T(8,128)(2,1)} %spectra.1, s32[128,128]{1,0:T(8,128)} %broadcast_in_dim.2.widths), custom_call_target="tpu_custom_call" | custom-call | tf_op jit(solution)/shard_map/pallas_call | solution.py:253
  238.8 4.8 %copy.4 = bf16[2,2,32,128,128]{4,3,2,1,0:T(8,128)(2,1)} copy(bf16[2,2,32,128,128]{4,3,2,1,0:T(8,128)(2,1)} %shard_map.28) | data formatting | bytes 8388608

commit v2 on v1

--- a/solution.py
+++ b/solution.py
@@ -7,17 +7,18 @@
 
 HMAX = 3
 ROUNDS = 2
-STEP = 2
+STEP = 1
 ROWS = 16
 LANES = 128
 
 
 def cross_kernel(
-    spectra, widths, out, energy, whitened, taken, own_tiles, sent_tiles,
-    halo_send, halo_recv, x_send, x_recv, t_send, t_recv, o_sem,
+    spectra_in, widths_in, out, spectra, widths, energy, whitened, taken, sent_tiles,
+    in_sem, halo_send, halo_recv, x_send, x_recv, t_send, t_recv,
 ):
     _, bins, channels, windows = spectra.shape
     half = bins // 2
+    middle = HMAX + STEP
     chunks = half // STEP
     fresh_chunks = (half - 2 * HMAX) // STEP
     first_edge_chunk = (half - HMAX) // STEP
@@ -118,12 +119,17 @@
             device_id_type=pl.DeviceIdType.MESH,
         )
 
-    def own_copy(r, chunk):
-        return pltpu.make_async_copy(
-            own_tiles.at[r, chunk],
-            out.at[r, :, pl.ds(chunk_start(mine, chunk), STEP)],
-            o_sem.at[r, chunk],
-        )
+    def load(start, count, index):
+        span = pl.ds(start, count)
+        return pltpu.make_async_copy(spectra_in.at[:, span], spectra.at[:, span], in_sem.at[index])
+
+    loads = (
+        load(half - middle, 2 * middle, 0),
+        load(given * (half + middle), half - middle, 1),
+        load(mine * (half + middle), half - middle, 2),
+    )
+    for copy in loads:
+        copy.start()
 
     barrier = pltpu.get_barrier_semaphore()
     for partner in partners:
@@ -143,13 +149,51 @@
             barrier, inc=1, device_id={"freq": freq + 1}, device_id_type=pl.DeviceIdType.MESH
         )
 
+    widths[...] = jnp.broadcast_to(
+        widths_in[...].astype(jnp.float32), (channels, LANES)
+    ).T
+
+    loads[0].wait()
+
+    @pl.loop(half - HMAX, half + HMAX)
+    def _(index):
+        make_energy(index)
+
+    def whiten_chunk(which, chunk):
+        start = chunk_start(which, chunk)
+
+        @pl.when(chunk < fresh_chunks)
+        def _():
+            for j in range(STEP):
+                make_energy(start + j + HMAX * (2 * which - 1))
+
+        @pl.when((chunk == first_edge_chunk) & (which == 0) & has_low)
+        def _():
+            halo_copy(1).wait_recv()
+
+        @pl.when((chunk == first_edge_chunk) & (which == 1) & has_high)
+        def _():
+            halo_copy(0).wait_recv()
+
+        for j in range(STEP):
+            whiten(start + j)
+
+    def give(chunk):
+        for r in range(ROUNDS):
+            spectra_copy(r, chunk).start()
+
+    whiten_chunk(given, 0)
+    pl.semaphore_wait(barrier, ROUNDS + has_low.astype(jnp.int32) + has_high.astype(jnp.int32))
+    give(0)
+
+    loads[1].wait()
+    loads[2].wait()
+
     @pl.loop(0, HMAX)
     def _(index):
         make_energy(index)
         make_energy(bins - HMAX + index)
 
-    pl.semaphore_wait(barrier, ROUNDS + has_low.astype(jnp.int32) + has_high.astype(jnp.int32))
-
     @pl.when(has_low)
     def _():
         halo_copy(0).start()
@@ -166,38 +210,14 @@
     def _():
         energy[pl.ds(bins + HMAX, HMAX)] = jnp.zeros((HMAX, channels, windows), jnp.float32)
 
-    @pl.loop(half - HMAX, half + HMAX)
-    def _(index):
-        make_energy(index)
-
-    def whiten_half(which, send):
-        @pl.loop(0, chunks)
-        def _(chunk):
-            start = chunk_start(which, chunk)
-
-            @pl.when(chunk < fresh_chunks)
-            def _():
-                for j in range(STEP):
-                    make_energy(start + j + HMAX * (2 * which - 1))
-
-            @pl.when((chunk == first_edge_chunk) & (which == 0) & has_low)
-            def _():
-                halo_copy(1).wait_recv()
-
-            @pl.when((chunk == first_edge_chunk) & (which == 1) & has_high)
-            def _():
-                halo_copy(0).wait_recv()
-
-            @pl.loop(0, STEP)
-            def _(j):
-                whiten(start + j)
-
-            if send:
-                for r in range(ROUNDS):
-                    spectra_copy(r, chunk).start()
-
-    whiten_half(given, True)
-    whiten_half(mine, False)
+    @pl.loop(1, chunks)
+    def _(chunk):
+        whiten_chunk(given, chunk)
+        give(chunk)
+
+    @pl.loop(0, chunks)
+    def _(chunk):
+        whiten_chunk(mine, chunk)
 
     @pl.loop(0, chunks)
     def _(chunk):
@@ -218,13 +238,12 @@
                 imag_sum = both[channels:, :channels] - both[:channels, channels:]
                 real_sum = real_sum * scale
                 imag_sum = imag_sum * scale
-                own_tiles[r, chunk, 0, j] = real_sum.astype(jnp.bfloat16)
-                own_tiles[r, chunk, 1, j] = imag_sum.astype(jnp.bfloat16)
+                out[r, 0, start + j] = real_sum.astype(jnp.bfloat16)
+                out[r, 1, start + j] = imag_sum.astype(jnp.bfloat16)
                 sent_tiles[r, chunk, 0, j] = real_sum.T.astype(jnp.bfloat16)
                 sent_tiles[r, chunk, 1, j] = (-imag_sum.T).astype(jnp.bfloat16)
 
             tile_copy(r, chunk, mine).start()
-            own_copy(r, chunk).start()
 
     @pl.when(has_low)
     def _():
@@ -238,7 +257,6 @@
     def _(chunk):
         for r in range(ROUNDS):
             spectra_copy(r, chunk).wait_send()
-            own_copy(r, chunk).wait()
             tile_copy(r, chunk, mine).wait_send()
             tile_copy(r, chunk, given).wait_recv()
 
@@ -247,30 +265,34 @@
     _, bins, channels, windows = spectra.shape
     half = bins // 2
     chunks = half // STEP
-    widths = jnp.broadcast_to(halfwidth[:, None], (channels, LANES))
+    widths = halfwidth.reshape(1, channels)
     tiles = (ROUNDS, chunks, 2, STEP, channels, channels)
     dma = pltpu.SemaphoreType.DMA
     return pl.pallas_call(
         cross_kernel,
-        out_shape=jax.ShapeDtypeStruct((ROUNDS, 2, bins, channels, channels), jnp.bfloat16),
-        in_specs=[pl.BlockSpec(memory_space=pltpu.VMEM)] * 2,
-        out_specs=pl.BlockSpec(memory_space=pl.ANY),
+        out_shape=pltpu.VMEM((ROUNDS, 2, bins, channels, channels), jnp.bfloat16),
+        in_specs=[
+            pl.BlockSpec(memory_space=pltpu.HBM),
+            pl.BlockSpec(memory_space=pltpu.VMEM),
+        ],
+        out_specs=pl.BlockSpec(memory_space=pltpu.VMEM),
         scratch_shapes=[
+            pltpu.VMEM((2, bins, channels, windows), jnp.bfloat16),
+            pltpu.VMEM((channels, LANES), jnp.float32),
             pltpu.VMEM((bins + 2 * HMAX, channels, windows), jnp.float32),
             pltpu.VMEM((2, bins, channels, windows), jnp.bfloat16),
             pltpu.VMEM((ROUNDS, 2, half, channels, windows), jnp.bfloat16),
             pltpu.VMEM(tiles, jnp.bfloat16),
-            pltpu.VMEM(tiles, jnp.bfloat16),
+            dma((3,)),
             dma((2,)),
             dma((2,)),
             dma((ROUNDS, chunks)),
             dma((ROUNDS, chunks)),
             dma((ROUNDS, chunks)),
             dma((ROUNDS, chunks)),
-            dma((ROUNDS, chunks)),
         ],
         compiler_params=pltpu.CompilerParams(
-            collective_id=0, has_side_effects=True, vmem_limit_bytes=56 * 2**20
+            collective_id=0, has_side_effects=True, vmem_limit_bytes=48 * 2**20
         ),
     )(spectra, widths)
 

time: 244 us -> 236 us (0.967)
  local copies, waits for them, and re-layouts: 6.15 us -> 2.67 us
  Pallas kernels: 237 us -> 234 us
    pallas_call x1, Pallas kernels: 237 us -> 234 us  [per_device(): pl.pallas_call(cross_kernel, out_shape=pltpu.VMEM((ROUNDS, 2, bins, chann...]
where the time goes in v2:
time: 236 us
  Pallas kernels  234 us (99%)
  local copies, waits for them, and re-layouts  2.67 us (1%)
    pallas_call x1, Pallas kernels, per_device(): pl.pallas_call(cross_kernel, out_shape=pltpu.VMEM((ROUNDS, 2, bins, chann...  234 us

profile of v2, /device:TPU:0, one launch (start us, length us, event | category | flops | bytes accessed | tf_op | source)
XLA Modules:
  0.0 236.2 jit_solution(9135888823459019754)
XLA Ops:
  0.0 0.0 copy-start
  0.0 0.7 copy-done
  0.7 233.5 %shard_map.28 = bf16[2,2,32,128,128]{4,3,2,1,0:T(8,128)(2,1)S(1)} custom-call(bf16[2,32,128,512]{3,2,1,0:T(8,128)(2,1)} %spectra_in.1, s32[1,128]{1,0:T(1,128)S(1)} %bitcast.1), custom_call_target="tpu_custom_call" | custom-call | tf_op jit(solution)/shard_map/pallas_call | solution.py:271
  234.2 2.0 copy.4
Async XLA Ops:
  0.0 0.7 copy-start

commit v3 on v2

--- a/solution.py
+++ b/solution.py
@@ -7,7 +7,8 @@
 
 HMAX = 3
 ROUNDS = 2
-STEP = 1
+STEP = 2
+PIECES = 4
 ROWS = 16
 LANES = 128
 
@@ -46,15 +47,15 @@
     def chunk_start(which, chunk):
         return (half - STEP * (chunk + 1)) + which * (STEP * (2 * chunk + 1))
 
-    def make_energy(k):
-        @pl.loop(0, row_blocks)
+    def make_energy(k, first=0, last=row_blocks):
+        @pl.loop(first, last)
         def _(block_index):
             rows = pl.ds(pl.multiple_of(block_index * ROWS, ROWS), ROWS)
             real_part = spectra[0, k, rows, :].astype(jnp.float32)
             imag_part = spectra[1, k, rows, :].astype(jnp.float32)
             energy[k + HMAX, rows, :] = real_part * real_part + imag_part * imag_part
 
-    def whiten(k):
+    def whiten(k, first=0, last=row_blocks):
         position = freq * bins + k
         inside = []
         for offset in range(1, HMAX + 1):
@@ -62,7 +63,7 @@
             high = (position + offset < bin_total).astype(jnp.int32)
             inside.append((low + high).astype(jnp.float32))
 
-        @pl.loop(0, row_blocks)
+        @pl.loop(first, last)
         def _(block_index):
             rows = pl.ds(pl.multiple_of(block_index * ROWS, ROWS), ROWS)
             width = widths[rows, :]
@@ -99,10 +100,10 @@
             device_id_type=pl.DeviceIdType.MESH,
         )
 
-    def spectra_copy(r, chunk):
+    def spectra_copy(r, chunk, rows=pl.ds(0, channels)):
         return pltpu.make_async_remote_copy(
-            src_ref=whitened.at[:, pl.ds(chunk_start(given, chunk), STEP)],
-            dst_ref=taken.at[r, :, pl.ds(chunk * STEP, STEP)],
+            src_ref=whitened.at[:, pl.ds(chunk_start(given, chunk), STEP), rows],
+            dst_ref=taken.at[r, :, pl.ds(chunk * STEP, STEP), rows],
             send_sem=x_send.at[r, chunk],
             recv_sem=x_recv.at[r, chunk],
             device_id={"blk": partners[r]},
@@ -119,17 +120,24 @@
             device_id_type=pl.DeviceIdType.MESH,
         )
 
-    def load(start, count, index):
+    def load(start, count, index, rows=pl.ds(0, channels)):
         span = pl.ds(start, count)
-        return pltpu.make_async_copy(spectra_in.at[:, span], spectra.at[:, span], in_sem.at[index])
-
-    loads = (
-        load(half - middle, 2 * middle, 0),
-        load(given * (half + middle), half - middle, 1),
-        load(mine * (half + middle), half - middle, 2),
-    )
-    for copy in loads:
-        copy.start()
+        return pltpu.make_async_copy(
+            spectra_in.at[:, span, rows], spectra.at[:, span, rows], in_sem.at[index]
+        )
+
+    def piece_rows(piece):
+        return pl.ds(pl.multiple_of(piece * (channels // PIECES), ROWS), channels // PIECES)
+
+    def load_piece(piece):
+        return load(half - middle, 2 * middle, piece, piece_rows(piece))
+
+    for piece in range(PIECES):
+        load_piece(piece).start()
+    load_given = load(given * (half + middle), half - middle, PIECES)
+    load_mine = load(mine * (half + middle), half - middle, PIECES + 1)
+    load_given.start()
+    load_mine.start()
 
     barrier = pltpu.get_barrier_semaphore()
     for partner in partners:
@@ -153,12 +161,6 @@
         widths_in[...].astype(jnp.float32), (channels, LANES)
     ).T
 
-    loads[0].wait()
-
-    @pl.loop(half - HMAX, half + HMAX)
-    def _(index):
-        make_energy(index)
-
     def whiten_chunk(which, chunk):
         start = chunk_start(which, chunk)
 
@@ -182,12 +184,33 @@
         for r in range(ROUNDS):
             spectra_copy(r, chunk).start()
 
-    whiten_chunk(given, 0)
+    def first_piece(piece):
+        first = piece * (row_blocks // PIECES)
+        last = first + row_blocks // PIECES
+        load_piece(piece).wait()
+
+        @pl.loop(0, 2 * HMAX + STEP)
+        def _(index):
+            make_energy(half - HMAX - STEP * (1 - given) + index, first, last)
+
+        for j in range(STEP):
+            whiten(chunk_start(given, 0) + j, first, last)
+
+    def give_piece(piece):
+        for r in range(ROUNDS):
+            spectra_copy(r, 0, piece_rows(piece)).start()
+
+    first_piece(0)
     pl.semaphore_wait(barrier, ROUNDS + has_low.astype(jnp.int32) + has_high.astype(jnp.int32))
-    give(0)
-
-    loads[1].wait()
-    loads[2].wait()
+    give_piece(0)
+
+    @pl.loop(1, PIECES)
+    def _(piece):
+        first_piece(piece)
+        give_piece(piece)
+
+    load_given.wait()
+    load_mine.wait()
 
     @pl.loop(0, HMAX)
     def _(index):
@@ -283,7 +306,7 @@
             pltpu.VMEM((2, bins, channels, windows), jnp.bfloat16),
             pltpu.VMEM((ROUNDS, 2, half, channels, windows), jnp.bfloat16),
             pltpu.VMEM(tiles, jnp.bfloat16),
-            dma((3,)),
+            dma((PIECES + 2,)),
             dma((2,)),
             dma((2,)),
             dma((ROUNDS, chunks)),

time: 236 us -> 236 us (level)
  no operation moved by 1% of the time
where the time goes in v3:
time: 236 us; the launch traced here: 235 us
  Pallas kernels  233 us (99%)
  local copies, waits for them, and re-layouts  2.67 us (1%)
    pallas_call x1, Pallas kernels, per_device(): pl.pallas_call(cross_kernel, out_shape=pltpu.VMEM((ROUNDS, 2, bins, chann...  233 us

profile of v3, /device:TPU:0, one launch (start us, length us, event | category | flops | bytes accessed | tf_op | source)
XLA Modules:
  0.0 235.4 jit_solution(15632685552814082279)
XLA Ops:
  0.0 0.0 copy-start
  0.0 0.7 copy-done
  0.7 232.7 %shard_map.28 = bf16[2,2,32,128,128]{4,3,2,1,0:T(8,128)(2,1)S(1)} custom-call(bf16[2,32,128,512]{3,2,1,0:T(8,128)(2,1)} %spectra_in.1, s32[1,128]{1,0:T(1,128)S(1)} %bitcast.1), custom_call_target="tpu_custom_call" | custom-call | tf_op jit(solution)/shard_map/pallas_call | solution.py:294
  233.4 2.0 copy.4
Async XLA Ops:
  0.0 0.7 copy-start

commit v4 on v3

--- a/solution.py
+++ b/solution.py
@@ -8,7 +8,7 @@
 HMAX = 3
 ROUNDS = 2
 STEP = 2
-PIECES = 4
+PIECES = 8
 ROWS = 16
 LANES = 128
 

time: 236 us -> 236 us (level)
  no operation moved by 1% of the time
where the time goes in v4:
time: 236 us
  Pallas kernels  233 us (99%)
  local copies, waits for them, and re-layouts  2.67 us (1%)
    pallas_call x1, Pallas kernels, per_device(): pl.pallas_call(cross_kernel, out_shape=pltpu.VMEM((ROUNDS, 2, bins, chann...  233 us

profile of v4, /device:TPU:0, one launch (start us, length us, event | category | flops | bytes accessed | tf_op | source)
XLA Modules:
  0.0 235.6 jit_solution(4163400894538814268)
XLA Ops:
  0.0 0.0 copy-start
  0.0 0.7 copy-done
  0.7 232.9 %shard_map.28 = bf16[2,2,32,128,128]{4,3,2,1,0:T(8,128)(2,1)S(1)} custom-call(bf16[2,32,128,512]{3,2,1,0:T(8,128)(2,1)} %spectra_in.1, s32[1,128]{1,0:T(1,128)S(1)} %bitcast.1), custom_call_target="tpu_custom_call" | custom-call | tf_op jit(solution)/shard_map/pallas_call | solution.py:294
  233.6 2.0 copy.4
Async XLA Ops:
  0.0 0.7 copy-start

commit v5 on v3

--- a/solution.py
+++ b/solution.py
@@ -284,6 +284,18 @@
             tile_copy(r, chunk, given).wait_recv()
 
 
+def store_kernel(tiles, out, sem):
+    copies = [
+        pltpu.make_async_copy(tiles.at[r, part], out.at[r, part], sem.at[r, part])
+        for r in range(ROUNDS)
+        for part in range(2)
+    ]
+    for copy in copies:
+        copy.start()
+    for copy in copies:
+        copy.wait()
+
+
 def per_device(spectra, halfwidth):
     _, bins, channels, windows = spectra.shape
     half = bins // 2
@@ -291,7 +303,7 @@
     widths = halfwidth.reshape(1, channels)
     tiles = (ROUNDS, chunks, 2, STEP, channels, channels)
     dma = pltpu.SemaphoreType.DMA
-    return pl.pallas_call(
+    crossed = pl.pallas_call(
         cross_kernel,
         out_shape=pltpu.VMEM((ROUNDS, 2, bins, channels, channels), jnp.bfloat16),
         in_specs=[
@@ -318,6 +330,13 @@
             collective_id=0, has_side_effects=True, vmem_limit_bytes=48 * 2**20
         ),
     )(spectra, widths)
+    return pl.pallas_call(
+        store_kernel,
+        out_shape=jax.ShapeDtypeStruct(crossed.shape, crossed.dtype),
+        in_specs=[pl.BlockSpec(memory_space=pltpu.VMEM)],
+        out_specs=pl.BlockSpec(memory_space=pltpu.HBM),
+        scratch_shapes=[dma((ROUNDS, 2))],
+    )(crossed)
 
 
 def solution(mesh):

time: 236 us -> 240 us (1.017)
  Pallas kernels: 233 us -> 237 us
    pallas_call x0 -> x1, Pallas kernels: none -> 4.23 us  [per_device(): pl.pallas_call(store_kernel, out_shape=jax.ShapeDtypeStruct(crossed.shape...]
where the time goes in v5:
time: 240 us
  Pallas kernels  237 us (99%)
  local copies, waits for them, and re-layouts  2.58 us (1%)
    pallas_call x1, Pallas kernels, per_device(): pl.pallas_call(cross_kernel, out_shape=pltpu.VMEM((ROUNDS, 2, bins, chann...  233 us

profile of v5, /device:TPU:0, one launch (start us, length us, event | category | flops | bytes accessed | tf_op | source)
XLA Modules:
  0.0 239.6 jit_solution(8332086797116267107)
XLA Ops:
  0.0 0.0 copy-start.1
  0.0 0.7 copy-done.1
  0.7 232.7 %shard_map.28.tiles = bf16[2,2,32,128,128]{4,3,2,1,0:T(8,128)(2,1)S(1)} custom-call(bf16[2,32,128,512]{3,2,1,0:T(8,128)(2,1)} %spectra_in.1, s32[1,128]{1,0:T(1,128)S(1)} %bitcast.1), custom_call_target="tpu_custom_call" | custom-call | tf_op jit(solution)/shard_map/pallas_call | solution.py:306
  233.4 0.0 copy-start
  233.4 1.9 copy-done
  235.3 4.2 %shard_map.29 = bf16[2,2,32,128,128]{4,3,2,1,0:T(8,128)(2,1)} custom-call(bf16[2,2,32,128,128]{4,3,2,1,0:T(8,128)(2,1)} %copy-done), custom_call_target="tpu_custom_call" | custom-call | tf_op jit(solution)/shard_map/pallas_call | solution.py:333
Async XLA Ops:
  0.0 0.7 copy-start.1
  233.4 1.9 copy-start
